TPU v7x, 256 devices: a whole 4x4x8 slice. The times are simulated.
256 devices in a mesh: tile: 16 (over z, core), lev: 4 (over x), tag: 4 (over y).
Axes of the slice: x: 4, y: 4, z: 8, core: 2. Of those that a mesh axis runs over, the one named last changes fastest.
Arguments:
- parent_field: float32 [8, 32, 256, 1024], P('tag', 'lev', 'tile'), may hold values from -6 to 6
- nest_field: float32 [8, 32, 256, 1024], P('tag', 'lev', 'tile'), may hold values from -6 to 6
- parent_mixing: float32 [32, 256, 1024], P('lev', 'tile'), may hold values from 0.05 to 5
- parent_eastward: float32 [256, 1024], P('tile'), may hold values from 0.02 to 0.12
- parent_northward: float32 [256, 1024], P('tile'), may hold values from 0.02 to 0.12
- nest_eastward: float32 [256, 1024], P('tile'), may hold values from 0.02 to 0.12
- nest_northward: float32 [256, 1024], P('tile'), may hold values from 0.02 to 0.12
- strip_tile: int32 [16, 256], replicated, may hold values from 0 to 15, as said below
- strip_block: int32 [16, 256], replicated, may hold values from 0 to 127
- strip_target: int32 [16, 256], replicated, may hold values from 0 to 127
- strip_count: int32 [16], replicated, may hold values from 1 to 256, as said below
Outputs:
- parent_adjoint: float32 [8, 32, 256, 1024], P('tag', 'lev', 'tile')
- nest_adjoint: float32 [8, 32, 256, 1024], P('tag', 'lev', 'tile')
- bulk_adjoint: float32 [32, 256, 1024], P('lev', 'tile', 'tag')
Inputs may be any that keep to these rules, and one draw needn't show every extreme that they name: `strip_tile`: among the first strip_count[j] entries of row j, every parent tile appears at most 16 times; in the row whose count is 256 every parent tile appears exactly 16 times. `strip_count`: exactly one nest tile lists 256 strips; every other lists at most 128.
All inputs are finite; a program needn't handle non-finite values.
Results may differ from a plain program's by a relative error of at most 0.0003.
Values sent between devices are 32-bit elements; how exact they have to be, the bound alone decides.
A program may use at most 64 MiB of HBM per device.

v0:
```python
import jax
import jax.numpy as jnp
from jax import lax
from jax.sharding import PartitionSpec as P

CAP = 16
NSUB = 3
HIGHEST = lax.Precision.HIGHEST


def extended(cells, sides, width):
    for axis, dim in sides:
        count = lax.axis_size(axis)
        ends = count - 1
        head = lax.slice_in_dim(cells, 0, width, axis=dim)
        tail = lax.slice_in_dim(cells, cells.shape[dim] - width, cells.shape[dim], axis=dim)
        cells = jnp.concatenate(
            [
                lax.ppermute(tail, axis, [(i, (i + 1) % count) for i in range(ends)]),
                cells,
                lax.ppermute(head, axis, [((i + 1) % count, i) for i in range(ends)]),
            ],
            axis=dim,
        )
    return cells


def tridiagonal(source, mixing):
    level_count = mixing.shape[0]
    mixing_up = jnp.concatenate([mixing[1:], jnp.zeros_like(mixing[:1])], axis=0)
    diagonal = 1.0 + mixing + mixing_up
    ratio_now = jnp.zeros_like(mixing[0])
    carry_now = jnp.zeros_like(source[:, 0])
    ratios = []
    carries = []
    for lev_index in range(level_count):
        pivot_now = diagonal[lev_index] + mixing[lev_index] * ratio_now
        ratio_now = -mixing_up[lev_index] / pivot_now
        carry_now = (source[:, lev_index] + mixing[lev_index] * carry_now) / pivot_now
        ratios.append(ratio_now)
        carries.append(carry_now)
    value_now = carries[level_count - 1]
    results = [value_now]
    for lev_index in range(level_count - 2, -1, -1):
        value_now = carries[lev_index] - ratios[lev_index] * value_now
        results.append(value_now)
    return jnp.stack(results[::-1], axis=1)


def relax(padded, eastward):
    center = padded[:-1, 1:-1]
    row_above = padded[:-1, :-2]
    row_below = padded[:-1, 2:]
    north_here = padded[-1, 1:-1]
    north_above = padded[-1, :-2]
    zero_column = jnp.zeros_like(center[:, :, :1])
    east_cell = jnp.concatenate([center[:, :, 1:], zero_column], axis=2)
    west_cell = jnp.concatenate([zero_column, center[:, :, :-1]], axis=2)
    west_rate = jnp.concatenate([jnp.zeros_like(eastward[:, :1]), eastward[:, :-1]], axis=1)
    return (
        center
        + north_here * (row_below - center)
        + north_above * (row_above - center)
        + eastward * (east_cell - center)
        + west_rate * (west_cell - center)
    )


def rims(stacked):
    return extended(stacked, (("tile", 1),), 1)


def advance(start, solved, parent_eastward, parent_northward, nest_eastward, nest_northward):
    tag_count, level_count, row_count, col_count = start.shape
    line_count = tag_count * level_count
    nest_now = start.reshape(line_count, row_count, col_count)
    parent_now = solved.reshape(line_count, row_count, col_count)
    for sub_step in range(NSUB):
        nest_stack = jnp.concatenate([nest_now, nest_northward[None]], axis=0)
        if sub_step == 0:
            parent_stack = jnp.concatenate([parent_now, parent_northward[None]], axis=0)
            padded = rims(jnp.concatenate([parent_stack, nest_stack], axis=0))
            parent_now = relax(padded[: line_count + 1], parent_eastward)
            nest_now = relax(padded[line_count + 1 :], nest_eastward)
        else:
            nest_now = relax(rims(nest_stack), nest_eastward)
    full_shape = (tag_count, level_count, row_count, col_count)
    return (parent_now.reshape(full_shape), nest_now.reshape(full_shape))


def deliver(parent_field, strip_tile, strip_block, strip_target, strip_count):
    tag_count, level_count, row_count, col_count = parent_field.shape
    line_count = tag_count * level_count
    block_count = row_count * col_count // 128
    tile_count, slot_total = strip_tile.shape
    own_index = lax.axis_index("tile")
    positions = jnp.arange(slot_total, dtype=jnp.int32)
    is_live = positions[None, :] < strip_count[:, None]
    from_here = jnp.logical_and(is_live, strip_tile == own_index).astype(jnp.int32)
    slot_rank = jnp.cumsum(from_here, axis=1) - 1
    slot_index = jnp.arange(CAP, dtype=jnp.int32)
    select = from_here[:, None, :] * (slot_rank[:, None, :] == slot_index[None, :, None]).astype(
        jnp.int32
    )
    source_block = jnp.sum(select * strip_block[:, None, :], axis=2).reshape(-1)
    filled = jnp.sum(select, axis=2).reshape(-1).astype(jnp.float32)
    blocks = parent_field.reshape(line_count, block_count, 128)
    packed = jnp.take(blocks, source_block, axis=1) * filled[None, :, None]
    received = lax.all_to_all(packed, "tile", split_axis=1, concat_axis=1, tiled=True)
    own_tile = lax.dynamic_index_in_dim(strip_tile, own_index, 0, keepdims=False)
    own_target = lax.dynamic_index_in_dim(strip_target, own_index, 0, keepdims=False)
    own_count = lax.dynamic_index_in_dim(strip_count, own_index, 0, keepdims=False)
    own_live = (positions < own_count).astype(jnp.int32)
    from_source = (own_tile[:, None] == jnp.arange(tile_count, dtype=jnp.int32)[None, :]).astype(
        jnp.int32
    ) * own_live[:, None]
    own_rank = jnp.sum((jnp.cumsum(from_source, axis=0) - 1) * from_source, axis=1)
    arrival = own_tile * CAP + own_rank
    pick_slot = (arrival[:, None] == jnp.arange(tile_count * CAP, dtype=jnp.int32)[None, :]).astype(
        jnp.float32
    )
    pick_slot = pick_slot * own_live[:, None].astype(jnp.float32)
    place_block = (own_target[:, None] == jnp.arange(block_count, dtype=jnp.int32)[None, :]).astype(
        jnp.float32
    )
    routing = jnp.dot(pick_slot.T, place_block, precision=HIGHEST)
    forcing = jnp.einsum("lic,ib->lbc", received, routing, precision=HIGHEST)
    return forcing.reshape(tag_count, level_count, row_count, col_count)


def shards(
    parent_field,
    nest_field,
    parent_mixing,
    parent_eastward,
    parent_northward,
    nest_eastward,
    nest_northward,
    strip_tile,
    strip_block,
    strip_target,
    strip_count,
):
    tag_count = parent_field.shape[0]
    forcing = deliver(parent_field, strip_tile, strip_block, strip_target, strip_count)
    stacked = jnp.concatenate([parent_field, parent_mixing[None]], axis=0)
    columns = lax.all_to_all(stacked, "lev", split_axis=3, concat_axis=1, tiled=True)
    column_result = tridiagonal(columns[:tag_count], columns[tag_count])
    solved = lax.all_to_all(column_result, "lev", split_axis=1, concat_axis=3, tiled=True)
    parent_adjoint, nest_adjoint = advance(
        nest_field + forcing,
        solved,
        parent_eastward,
        parent_northward,
        nest_eastward,
        nest_northward,
    )
    bulk_adjoint = lax.psum_scatter(
        jnp.sum(parent_adjoint, axis=0), "tag", scatter_dimension=2, tiled=True
    )
    return (parent_adjoint, nest_adjoint, bulk_adjoint)


def solution(mesh):
    in_specs = (
        P("tag", "lev", "tile", None),
        P("tag", "lev", "tile", None),
        P("lev", "tile", None),
        P("tile", None),
        P("tile", None),
        P("tile", None),
        P("tile", None),
        P(),
        P(),
        P(),
        P(),
    )
    out_specs = (
        P("tag", "lev", "tile", None),
        P("tag", "lev", "tile", None),
        P("lev", "tile", "tag"),
    )
    return jax.shard_map(shards, mesh=mesh, in_specs=in_specs, out_specs=out_specs, check_vma=False)
```

profile of v0, /device:TPU:2, one launch (start us, length us, event | category | flops | bytes accessed | tf_op | source)
XLA Modules:
  0.0 209.8 jit_solution(3081090923372214536)
XLA Ops:
  7.2 1.5 pad_maximum_fusion.5
  8.7 6.9 %copy.55 = f32[3,8,16,1024]{2,1,0,3:T(8,128)} copy(f32[3,8,16,1024]{3,2,1,0:T(8,128)S(1)} %pad_maximum_fusion.5) | data formatting | bytes 3145728 | tf_op jit(solution)/shard_map/concatenate | solution.py:146
  15.6 8.3 %reshape.176 = f32[4,1,98304]{2,1,0:T(1,128)} reshape(f32[1024,3,8,16]{3,2,1,0:T(8,128)} %bitcast.230) | data formatting | bytes 3145728
  23.9 5.9 %all-to-all-start = ((f32[4,1,98304]{2,1,0:T(1,128)}), f32[4,1,98304]{2,1,0:T(1,128)S(1)}, u32[]{:S(2)}, u32[]{:S(2)}) async-start(f32[4,1,98304]{2,1,0:T(1,128)} %reshape.176), calls=%async_computation | async-start | bytes 3145728 | tf_op jit(solution)/shard_map/all_to_all | solution.py:147
  29.8 1.1 reshape.159
  31.0 0.6 reduce-window.16
  31.6 0.2 slice_reduce_fusion
  32.0 0.6 select_reduce_fusion
  32.7 1.8 copy.65
  34.7 13.4 %all-to-all-done = f32[4,1,98304]{2,1,0:T(1,128)S(1)} async-done(((f32[4,1,98304]{2,1,0:T(1,128)}), f32[4,1,98304]{2,1,0:T(1,128)S(1)}, u32[]{:S(2)}, u32[]{:S(2)}) %all-to-all-start) | async-done | bytes 1572896 | tf_op jit(solution)/shard_map/all_to_all | solution.py:147
  48.1 1.2 copy-done.1
  49.2 0.5 broadcast.2764
  49.8 6.2 %reduce.4 = f32[4,98304]{1,0:T(4,128)S(1)} reduce(f32[4,1,98304]{2,1,0:T(1,128)} %copy-done.1, f32[]{:T(128)} %broadcast.2764), dimensions={1}, to_apply=%all_to_all.25.reduce_sub_computation | reduce | bytes 3145732 | tf_op jit(solution)/shard_map/all_to_all | solution.py:147
  55.9 8.9 %reshape.177 = f32[1024,3,8,16]{3,2,1,0:T(8,128)} reshape(f32[4,98304]{1,0:T(4,128)S(1)} %reduce.4) | data formatting | bytes 3145728
  64.8 7.8 %copy.69 = f32[3,8,16,4,256]{4,3,2,1,0:T(4,128)S(1)} copy(f32[3,8,16,4,256]{2,1,0,4,3:T(8,128)} %bitcast.231) | data formatting | bytes 3145728 | tf_op jit(solution)/shard_map/all_to_all | solution.py:147
  72.7 0.1 copy.58
  72.9 0.2 slice.659
  73.6 0.2 copy.57
  74.0 0.4 constant_dynamic-update-slice_fusion.31
  74.9 1.0 copy.59
  75.9 5.7 %all-to-all-start.1 = ((f32[2,32,16,256]{3,2,0,1:T(8,128)}), f32[2,32,16,256]{3,2,0,1:T(8,128)}, u32[]{:S(2)}, u32[]{:S(2)}) async-start(f32[2,32,16,256]{3,2,0,1:T(8,128)} %copy.59), calls=%async_computation.1 | async-start | bytes 2097152 | tf_op jit(solution)/shard_map/all_to_all | solution.py:149
  81.6 1.0 gather_fusion
  82.6 2.5 %multiply_bitcast_fusion = f32[16,256,128]{2,0,1:T(8,128)} fusion(f32[256,16,128]{2,1,0:T(8,128)S(1)} %gather_fusion, f32[256]{0:T(256)S(1)} %convert_element_type.43, pred[256]{0:T(512)(128)(4,1)S(1)} %compare_and_fusion), kind=kLoop, calls=%fused_computation.5 | loop fusion | flops 1048576 | bytes 4195584 | tf_op jit(solution)/shard_map/mul | solution.py:108
  85.2 8.3 %all-to-all-done.1 = f32[2,32,16,256]{3,2,0,1:T(8,128)} async-done(((f32[2,32,16,256]{3,2,0,1:T(8,128)}), f32[2,32,16,256]{3,2,0,1:T(8,128)}, u32[]{:S(2)}, u32[]{:S(2)}) %all-to-all-start.1) | async-done | bytes 1048608 | tf_op jit(solution)/shard_map/all_to_all | solution.py:149
  93.4 9.6 %all-to-all-start.2 = ((f32[16,256,128]{2,0,1:T(8,128)}), f32[16,256,128]{2,0,1:T(8,128)}, u32[]{:S(2)}, u32[]{:S(2)}) async-start(f32[16,256,128]{2,0,1:T(8,128)} %multiply_bitcast_fusion), calls=%async_computation.2 | async-start | bytes 4194304 | tf_op jit(solution)/shard_map/all_to_all | solution.py:109
  103.1 0.6 dynamic_slice.12
  103.7 0.7 compare_convert_fusion.1
  104.3 0.7 constant_dynamic-slice_fusion
  105.1 0.6 reduce-window.14
  105.6 0.2 slice_reduce_fusion.1
  106.0 0.7 compare_convert_fusion
  106.7 0.7 fusion.86
  107.5 0.4 convolution_bitcast_fusion
  107.9 1.9 copy.61
  109.8 0.5 reshape.154
  110.4 1.7 fusion.137
  112.1 40.2 %all-to-all-done.2 = f32[16,256,128]{2,0,1:T(8,128)} async-done(((f32[16,256,128]{2,0,1:T(8,128)}), f32[16,256,128]{2,0,1:T(8,128)}, u32[]{:S(2)}, u32[]{:S(2)}) %all-to-all-start.2) | async-done | bytes 2097184 | tf_op jit(solution)/shard_map/all_to_all | solution.py:109
  152.3 3.4 %fusion.4 = f32[16,128,128]{2,1,0:T(8,128)S(1)} fusion(f32[256,128,1]{0,1,2:T(8,128)S(1)} %convolution_bitcast_fusion, f32[16,256,128]{2,0,1:T(8,128)} %all-to-all-done.2), kind=kOutput, calls=%fused_computation.12 | convolution fusion | flops 805306368 | bytes 3276800 | tf_op jit(solution)/shard_map/lic,ib->lbc/dot_general | solution.py:127
  155.7 0.2 reshape.161
  155.9 1.4 add.2442
  157.3 0.2 pad_maximum_fusion.15
  157.5 2.1 collective-permute-start.1
  159.6 1.3 collective-permute-start
  160.9 0.4 fusion.136
  161.3 1.5 collective-permute-done
  162.9 0.7 fusion.13
  163.6 1.7 fusion.135
  165.3 0.1 fusion.44
  165.4 5.2 %collective-permute-start.3 = (f32[17,1,1024]{2,1,0:T(1,128)S(1)}, f32[17,1,1024]{2,1,0:T(1,128)S(1)}, u32[]{:S(2)}, u32[]{:S(2)}) collective-permute-start(f32[17,1,1024]{2,1,0:T(1,128)S(1)} %get-tuple-element.88), channel_id=1, source_target_pairs={{0,16},{16,32},{32,48},{48,64},{64,80},{80,96},{96,112},{112,128},... | collective-permute-start | bytes 208904 | tf_op jit(solution)/shard_map/ppermute | solution.py:19
  170.7 1.5 collective-permute-start.2
  172.2 1.7 fusion.35
  173.9 2.1 %reduce_sum.39 = f32[8,16,1024]{2,1,0:T(8,128)} reduce(f32[2,8,16,1024]{3,2,1,0:T(8,128)} %bitcast.265, f32[]{:T(128)} %constant.48.clone.1), dimensions={0}, to_apply=%region_7.8 | reduce | flops 131072 | bytes 1572868 | tf_op jit(solution)/shard_map/reduce_sum | solution.py:159
  176.1 0.3 fusion.2
  176.4 0.9 copy-done.3
  177.3 0.3 copy-done.4
  177.6 0.6 fusion.20
  178.2 0.1 fusion.43
  178.4 3.0 %collective-permute-start.5 = (f32[17,1,1024]{2,1,0:T(1,128)S(1)}, f32[17,1,1024]{2,1,0:T(1,128)S(1)}, u32[]{:S(2)}, u32[]{:S(2)}) collective-permute-start(f32[17,1,1024]{2,1,0:T(1,128)S(1)} %get-tuple-element.86), channel_id=1, source_target_pairs={{0,16},{16,32},{32,48},{48,64},{64,80},{80,96},{96,112},{112,128},... | collective-permute-start | bytes 208904 | tf_op jit(solution)/shard_map/ppermute | solution.py:19
  181.4 0.4 fusion.134
  181.8 1.3 collective-permute-start.4
  183.1 0.3 fusion.3
  183.4 2.3 %collective-permute-done.4 = f32[17,1,1024]{2,1,0:T(1,128)S(1)} collective-permute-done((f32[17,1,1024]{2,1,0:T(1,128)S(1)}, f32[17,1,1024]{2,1,0:T(1,128)S(1)}, u32[]{:S(2)}, u32[]{:S(2)}) %collective-permute-start.4) | collective-permute-done | bytes 69664 | tf_op jit(solution)/shard_map/ppermute | solution.py:21
  185.7 1.6 fusion.27
  187.3 15.6 %reduce-scatter.2.cloned.1.call-done = f32[8,16,256]{2,1,0:T(8,128)} async-done(((f32[8,16,1024]{2,1,0:T(8,128)}), f32[8,16,256]{2,1,0:T(8,128)}) %reduce-scatter.2.cloned.1.call-update) | async-done | bytes 131088 | tf_op jit(solution)/shard_map/reduce_scatter | solution.py:158
  (102 shorter events, 1.8 us)
Async XLA Ops:
  23.9 5.9 %copy-start.2 = (f32[2,8,16,1024]{3,2,1,0:T(8,128)S(1)}, f32[2,8,16,1024]{3,2,1,0:T(8,128)}, u32[]{:S(2)}) copy-start(f32[2,8,16,1024]{3,2,1,0:T(8,128)} %param.11) | copy-start | bytes 3145732
  23.9 24.2 %all-to-all-start = ((f32[4,1,98304]{2,1,0:T(1,128)}), f32[4,1,98304]{2,1,0:T(1,128)S(1)}, u32[]{:S(2)}, u32[]{:S(2)}) async-start(f32[4,1,98304]{2,1,0:T(1,128)} %reshape.176), calls=%async_computation | async-start | bytes 3145728 | tf_op jit(solution)/shard_map/all_to_all | solution.py:147
  29.8 1.1 copy-start.10
  29.8 1.1 copy-start.12
  29.8 2.2 %copy-start.11 = (s32[16,256]{1,0:T(8,128)S(1)}, s32[16,256]{1,0:T(8,128)}, u32[]{:S(2)}) copy-start(s32[16,256]{1,0:T(8,128)} %param.19) | copy-start | bytes 49156
  48.1 1.2 copy-start.1
  75.9 17.5 %all-to-all-start.1 = ((f32[2,32,16,256]{3,2,0,1:T(8,128)}), f32[2,32,16,256]{3,2,0,1:T(8,128)}, u32[]{:S(2)}, u32[]{:S(2)}) async-start(f32[2,32,16,256]{3,2,0,1:T(8,128)} %copy.59), calls=%async_computation.1 | async-start | bytes 2097152 | tf_op jit(solution)/shard_map/all_to_all | solution.py:149
  85.2 20.7 %copy-start.8 = (f32[16,1024]{1,0:T(8,128)S(1)}, f32[16,1024]{1,0:T(8,128)}, u32[]{:S(2)}) copy-start(f32[16,1024]{1,0:T(8,128)} %param.16) | copy-start | bytes 196612
  85.2 20.8 %copy-start.9 = (f32[16,1024]{1,0:T(8,128)S(1)}, f32[16,1024]{1,0:T(8,128)}, u32[]{:S(2)}) copy-start(f32[16,1024]{1,0:T(8,128)} %param.14) | copy-start | bytes 196612
  93.4 58.9 %all-to-all-start.2 = ((f32[16,256,128]{2,0,1:T(8,128)}), f32[16,256,128]{2,0,1:T(8,128)}, u32[]{:S(2)}, u32[]{:S(2)}) async-start(f32[16,256,128]{2,0,1:T(8,128)} %multiply_bitcast_fusion), calls=%async_computation.2 | async-start | bytes 4194304 | tf_op jit(solution)/shard_map/all_to_all | solution.py:109
  103.0 99.9 %reduce-scatter.2.cloned.1.call-start = ((), (), s32[]{:S(2)}) async-start(), calls=%async_computation.4 | async-start | bytes 655360 | tf_op jit(solution)/shard_map/reduce_scatter | solution.py:158
  155.8 1.4 copy-start
  155.8 1.4 copy-start.7
  157.5 3.8 %collective-permute-start.1 = (f32[34,1,1024]{2,1,0:T(1,128)S(1)}, f32[34,1,1024]{2,1,0:T(1,128)S(1)}, u32[]{:S(2)}, u32[]{:S(2)}) collective-permute-start(f32[34,1,1024]{2,1,0:T(1,128)S(1)} %get-tuple-element.84), channel_id=1, source_target_pairs={{0,16},{16,32},{32,48},{48,64},{64,80},{80,96},{96,112},{112,128},... | collective-permute-start | bytes 417800 | tf_op jit(solution)/shard_map/ppermute | solution.py:19
  159.6 3.3 %collective-permute-start = (f32[34,1,1024]{2,1,0:T(1,128)S(1)}, f32[34,1,1024]{2,1,0:T(1,128)S(1)}, u32[]{:S(2)}, u32[]{:S(2)}) collective-permute-start(f32[34,1,1024]{2,1,0:T(1,128)S(1)} %get-tuple-element.83), channel_id=1, source_target_pairs={{16,0},{32,16},{48,32},{64,48},{80,64},{96,80},{112,96},{128,112},... | collective-permute-start | bytes 417800 | tf_op jit(solution)/shard_map/ppermute | solution.py:21
  163.6 8.6 %copy-start.6 = (f32[16,16,1023]{2,1,0:T(8,128)S(1)}, f32[16,16,1023]{2,1,0:T(8,128)}, u32[]{:S(2)}) copy-start(f32[16,16,1023]{2,1,0:T(8,128)} %get-tuple-element.96) | copy-start | bytes 3142660
  165.3 6.9 %copy-start.5 = (f32[16,16,1023]{2,1,0:T(8,128)S(1)}, f32[16,16,1023]{2,1,0:T(8,128)}, u32[]{:S(2)}) copy-start(f32[16,16,1023]{2,1,0:T(8,128)} %get-tuple-element.95) | copy-start | bytes 3142660
  165.4 10.7 %collective-permute-start.3 = (f32[17,1,1024]{2,1,0:T(1,128)S(1)}, f32[17,1,1024]{2,1,0:T(1,128)S(1)}, u32[]{:S(2)}, u32[]{:S(2)}) collective-permute-start(f32[17,1,1024]{2,1,0:T(1,128)S(1)} %get-tuple-element.88), channel_id=1, source_target_pairs={{0,16},{16,32},{32,48},{48,64},{64,80},{80,96},{96,112},{112,128},... | collective-permute-start | bytes 208904 | tf_op jit(solution)/shard_map/ppermute | solution.py:19
  170.7 5.7 %collective-permute-start.2 = (f32[17,1,1024]{2,1,0:T(1,128)S(1)}, f32[17,1,1024]{2,1,0:T(1,128)S(1)}, u32[]{:S(2)}, u32[]{:S(2)}) collective-permute-start(f32[17,1,1024]{2,1,0:T(1,128)S(1)} %get-tuple-element.87), channel_id=1, source_target_pairs={{16,0},{32,16},{48,32},{64,48},{80,64},{96,80},{112,96},{128,112},... | collective-permute-start | bytes 208904 | tf_op jit(solution)/shard_map/ppermute | solution.py:21
  176.1 1.2 copy-start.3
  176.1 1.5 copy-start.4
  178.4 4.7 %collective-permute-start.5 = (f32[17,1,1024]{2,1,0:T(1,128)S(1)}, f32[17,1,1024]{2,1,0:T(1,128)S(1)}, u32[]{:S(2)}, u32[]{:S(2)}) collective-permute-start(f32[17,1,1024]{2,1,0:T(1,128)S(1)} %get-tuple-element.86), channel_id=1, source_target_pairs={{0,16},{16,32},{32,48},{48,64},{64,80},{80,96},{96,112},{112,128},... | collective-permute-start | bytes 208904 | tf_op jit(solution)/shard_map/ppermute | solution.py:19
  181.8 3.9 %collective-permute-start.4 = (f32[17,1,1024]{2,1,0:T(1,128)S(1)}, f32[17,1,1024]{2,1,0:T(1,128)S(1)}, u32[]{:S(2)}, u32[]{:S(2)}) collective-permute-start(f32[17,1,1024]{2,1,0:T(1,128)S(1)} %get-tuple-element.85), channel_id=1, source_target_pairs={{16,0},{32,16},{48,32},{64,48},{80,64},{96,80},{112,96},{128,112},... | collective-permute-start | bytes 208904 | tf_op jit(solution)/shard_map/ppermute | solution.py:21
Sparse Core Ops, SparseCore 0:
  176.2 26.7 reduce-scatter.1
where the time goes:
time: 211 us; the launch traced here: 210 us
  waiting for transfers between devices  81.3 us (39%)
  local copies, waits for them, and re-layouts  49.5 us (23%)
  starting transfers between devices  35.7 us (17%)
  other arithmetic  24.7 us (12%)
  between operations  14.8 us (7%)
  matrix products  3.79 us (2%)
    all_to_all x1, waiting for transfers between devices, deliver(): lax.all_to_all(packed, 'tile', split_axis=1, concat_axis=1, tiled=True)  40.2 us
    unnamed x43, local copies, waits for them, and re-layouts  19.7 us
    reduce_scatter x1, waiting for transfers between devices, shards(): lax.psum_scatter(jnp.sum(parent_adjoint, axis=0), 'tag', scatter_dimensio...  15.6 us
    all_to_all x1, waiting for transfers between devices, shards(): lax.all_to_all(stacked, 'lev', split_axis=3, concat_axis=1, tiled=True)  13.4 us
    ppermute x3, starting transfers between devices, extended(): lax.ppermute(tail, axis, [(i, (i + 1) % count) for i in range(ends)])  10.3 us
    all_to_all x1, starting transfers between devices, deliver(): lax.all_to_all(packed, 'tile', split_axis=1, concat_axis=1, tiled=True)  9.61 us
    all_to_all x2, local copies, waits for them, and re-layouts, shards(): lax.all_to_all(stacked, 'lev', split_axis=3, concat_axis=1, tiled=True)  8.35 us
    all_to_all x1, waiting for transfers between devices, shards(): lax.all_to_all(column_result, 'lev', split_axis=1, concat_axis=3, tiled=T...  8.27 us
  transfers between devices with their start and end apart: 10, of which 6 were waited for; matrix products, arithmetic and copies ran while one was open for 12% of the time, Pallas kernels for 0%

commit v1 on v0

--- a/solution.py
+++ b/solution.py
@@ -144,7 +144,18 @@
     tag_count = parent_field.shape[0]
     forcing = deliver(parent_field, strip_tile, strip_block, strip_target, strip_count)
     stacked = jnp.concatenate([parent_field, parent_mixing[None]], axis=0)
-    columns = lax.all_to_all(stacked, "lev", split_axis=3, concat_axis=1, tiled=True)
+    w_next, carry = (jax.lax.psum(1, axis_name="lev"), jax.lax.axis_index("lev"))
+    shaped = stacked.shape[3] // w_next
+    passed = list(stacked.shape)
+    passed[3] = shaped
+    big = passed[1]
+    passed[1] = big * w_next
+    columns = jnp.zeros(passed, stacked.dtype)
+    for t in range(w_next):
+        tall = lax.dynamic_slice_in_dim(stacked, (carry ^ t) * shaped, shaped, axis=3)
+        if t:
+            tall = jax.lax.ppermute(tall, axis_name="lev", perm=[(w, w ^ t) for w in range(w_next)])
+        columns = lax.dynamic_update_slice_in_dim(columns, tall, (carry ^ t) * big, axis=1)
     column_result = tridiagonal(columns[:tag_count], columns[tag_count])
     solved = lax.all_to_all(column_result, "lev", split_axis=1, concat_axis=3, tiled=True)
     parent_adjoint, nest_adjoint = advance(

time: 211 us -> 189 us (0.90)
  local copies, waits for them, and re-layouts: 49.5 us -> 34.3 us
  waiting for transfers between devices: 81.3 us -> 71.7 us
  other arithmetic: 24.7 us -> 31.2 us
  starting transfers between devices: 35.7 us -> 33.1 us
    all_to_all x1 -> x0, waiting for transfers between devices: 13.4 us -> none  [shards(): lax.all_to_all(stacked, 'lev', split_axis=3, concat_axis=1, tiled=True)]
    unnamed x16, other arithmetic: 0.53 us -> 10.5 us
    all_to_all x2 -> x0, local copies, waits for them, and re-layouts: 8.35 us -> none  [shards(): lax.all_to_all(stacked, 'lev', split_axis=3, concat_axis=1, tiled=True)]
    ppermute x0 -> x3, waiting for transfers between devices: none -> 7.98 us  [shards(): jax.lax.ppermute(tall, axis_name='lev', perm=[(w, w ^ t) for w in range(w...]
    unnamed x43 -> x49, local copies, waits for them, and re-layouts: 19.7 us -> 12.7 us
    concatenate x1 -> x0, local copies, waits for them, and re-layouts: 6.92 us -> none  [shards(): stacked = jnp.concatenate([parent_field, parent_mixing[None]], axis=0)]
    all_to_all x1 -> x0, other arithmetic: 6.16 us -> none  [shards(): lax.all_to_all(stacked, 'lev', split_axis=3, concat_axis=1, tiled=True)]
    all_to_all x1 -> x0, starting transfers between devices: 5.93 us -> none  [shards(): lax.all_to_all(stacked, 'lev', split_axis=3, concat_axis=1, tiled=True)]
  transfers between devices with their start and end apart: 10 -> 12, of which waited for: 6 -> 7; matrix products, arithmetic and copies ran while one was open for 12% -> 18% of each run, Pallas kernels for 0% -> 0%
where the time goes in v1:
time: 189 us; the launch traced here: 188 us
  waiting for transfers between devices  71.7 us (38%)
  local copies, waits for them, and re-layouts  34.3 us (18%)
  starting transfers between devices  33.1 us (18%)
  other arithmetic  31.2 us (17%)
  between operations  14.6 us (8%)
  matrix products  3.2 us (2%)
    all_to_all x1, waiting for transfers between devices, deliver(): lax.all_to_all(packed, 'tile', split_axis=1, concat_axis=1, tiled=True)  38 us
    reduce_scatter x1, waiting for transfers between devices, shards(): lax.psum_scatter(jnp.sum(parent_adjoint, axis=0), 'tag', scatter_dimensio...  15.6 us
    unnamed x49, local copies, waits for them, and re-layouts  12.7 us
    unnamed x16, other arithmetic  10.5 us
    ppermute x3, starting transfers between devices, extended(): lax.ppermute(tail, axis, [(i, (i + 1) % count) for i in range(ends)])  10.4 us
    all_to_all x1, starting transfers between devices, deliver(): lax.all_to_all(packed, 'tile', split_axis=1, concat_axis=1, tiled=True)  8.57 us
    ppermute x3, waiting for transfers between devices, shards(): jax.lax.ppermute(tall, axis_name='lev', perm=[(w, w ^ t) for w in range(w...  7.98 us
    all_to_all x1, starting transfers between devices, shards(): lax.all_to_all(column_result, 'lev', split_axis=1, concat_axis=3, tiled=T...  6.5 us
  transfers between devices with their start and end apart: 12, of which 7 were waited for; matrix products, arithmetic and copies ran while one was open for 18% of the time, Pallas kernels for 0%

profile of v1, /device:TPU:2, one launch (start us, length us, event | category | flops | bytes accessed | tf_op | source)
XLA Modules:
  0.0 188.2 jit_solution(9808596055891404108)
XLA Ops:
  7.4 0.8 copy-done.9
  8.6 1.1 fusion.41
  9.6 2.3 %collective-permute-start = (f32[3,8,16,256]{3,2,0,1:T(8,128)}, f32[3,8,16,256]{3,2,0,1:T(8,128)}, u32[]{:S(2)}, u32[]{:S(2)}) collective-permute-start(f32[3,8,16,256]{3,2,0,1:T(8,128)} %get-tuple-element.136), channel_id=1, source_target_pairs={{0,4},{4,0},{8,12},{12,8},{1,5},{5,1},{9,13},{13,9},{2,6},{6,2},{1... | collective-permute-start | bytes 1179656 | tf_op jit(solution)/shard_map/ppermute | solution.py:157
  11.9 0.7 collective-permute-start.1
  12.6 0.8 collective-permute-start.2
  13.4 0.7 copy_bitcast_fusion.1
  15.0 0.7 fusion.123
  15.7 1.1 reshape.2623
  17.5 0.7 reshape.2624
  18.1 0.7 reshape.2622
  18.8 1.8 copy.107
  20.6 0.7 convert_element_type.43
  21.3 1.0 collective-permute-done
  22.2 1.0 constant_dynamic-update-slice_fusion.34
  23.3 7.0 %collective-permute-done.1 = f32[3,8,16,256]{3,2,0,1:T(8,128)} collective-permute-done((f32[3,8,16,256]{3,2,0,1:T(8,128)}, f32[3,8,16,256]{3,2,0,1:T(8,128)}, u32[]{:S(2)}, u32[]{:S(2)}) %collective-permute-start.1) | collective-permute-done | bytes 393248 | tf_op jit(solution)/shard_map/ppermute | solution.py:157
  30.3 1.0 constant_dynamic-update-slice_fusion.33
  32.1 1.2 constant_dynamic-update-slice_fusion.31
  33.9 0.6 constant_dynamic-update-slice_fusion.29
  35.1 0.6 constant_dynamic-update-slice_fusion.27
  36.4 0.6 constant_dynamic-update-slice_fusion.25
  37.6 0.6 constant_dynamic-update-slice_fusion.23
  38.8 0.6 constant_dynamic-update-slice_fusion.21
  40.1 0.6 constant_dynamic-update-slice_fusion.19
  41.3 0.6 constant_dynamic-update-slice_fusion.17
  42.6 0.6 constant_dynamic-update-slice_fusion.15
  43.8 0.6 constant_dynamic-update-slice_fusion.13
  45.0 0.6 constant_dynamic-update-slice_fusion.11
  46.3 0.6 constant_dynamic-update-slice_fusion.9
  47.5 0.6 constant_dynamic-update-slice_fusion.7
  51.2 0.6 constant_dynamic-update-slice_fusion.1
  51.9 0.6 constant_dynamic-update-slice_fusion
  52.5 6.5 %all-to-all-start = ((f32[2,32,16,256]{3,2,0,1:T(8,128)}), f32[2,32,16,256]{3,2,0,1:T(8,128)S(1)}, u32[]{:S(2)}, u32[]{:S(2)}) async-start(f32[2,32,16,256]{3,2,0,1:T(8,128)} %constant_dynamic-update-slice_fusion), calls=%async_computation | async-start | bytes 2097152 | tf_op jit(solution)/shard_map/all_to_all | solution.py:160
  59.0 2.4 %gather_fusion = f32[256,16,128]{2,1,0:T(8,128)} fusion(f32[16,128,128]{2,0,1:T(8,128)S(1)} %copy.107, s32[1024]{0:T(1024)S(1)} %pad_clamp_fusion), kind=kCustom, calls=%fused_computation | custom fusion | bytes 4195328 | tf_op jit(solution)/shard_map/jit(_take)/gather | solution.py:108
  61.4 3.7 %multiply_bitcast_fusion = f32[16,256,128]{2,0,1:T(8,128)} fusion(f32[256,16,128]{2,1,0:T(8,128)} %gather_fusion, f32[256]{0:T(256)S(1)} %copy-done.13, pred[256]{0:T(512)(128)(4,1)S(1)} %compare_and_fusion), kind=kLoop, calls=%fused_computation.9 | loop fusion | flops 1048576 | bytes 4195584 | tf_op jit(solution)/shard_map/mul | solution.py:108
  65.1 6.3 %all-to-all-done = f32[2,32,16,256]{3,2,0,1:T(8,128)S(1)} async-done(((f32[2,32,16,256]{3,2,0,1:T(8,128)}), f32[2,32,16,256]{3,2,0,1:T(8,128)S(1)}, u32[]{:S(2)}, u32[]{:S(2)}) %all-to-all-start) | async-done | bytes 1048608 | tf_op jit(solution)/shard_map/all_to_all | solution.py:160
  71.4 1.0 copy-done.2
  72.4 8.6 %all-to-all-start.1 = ((f32[16,256,128]{2,0,1:T(8,128)}), f32[16,256,128]{2,0,1:T(8,128)S(1)}, u32[]{:S(2)}, u32[]{:S(2)}) async-start(f32[16,256,128]{2,0,1:T(8,128)} %multiply_bitcast_fusion), calls=%async_computation.1 | async-start | bytes 4194304 | tf_op jit(solution)/shard_map/all_to_all | solution.py:109
  81.6 0.7 compare_convert_fusion.1
  82.3 0.7 constant_dynamic-slice_fusion
  84.0 0.7 fusion.126
  84.7 0.7 compare_convert_fusion
  85.8 2.9 %copy.103 = f32[2,8,16,4,256]{4,3,2,1,0:T(4,128)} copy(f32[2,8,16,4,256]{4,2,0,1,3:T(8,128)} %bitcast.738) | data formatting | bytes 2097152 | tf_op jit(solution)/shard_map/all_to_all | solution.py:160
  88.7 1.8 reshape.2618
  90.5 1.7 fusion.177
  92.2 38.0 %all-to-all-done.1 = f32[16,256,128]{2,0,1:T(8,128)S(1)} async-done(((f32[16,256,128]{2,0,1:T(8,128)}), f32[16,256,128]{2,0,1:T(8,128)S(1)}, u32[]{:S(2)}, u32[]{:S(2)}) %all-to-all-start.1) | async-done | bytes 2097184 | tf_op jit(solution)/shard_map/all_to_all | solution.py:109
  130.2 2.8 %fusion.4 = f32[16,128,128]{2,1,0:T(8,128)} fusion(f32[256,128,1]{0,1,2:T(8,128)S(1)} %convolution_bitcast_fusion, f32[16,256,128]{2,0,1:T(8,128)S(1)} %all-to-all-done.1), kind=kOutput, calls=%fused_computation.19 | convolution fusion | flops 805306368 | bytes 3276800 | tf_op jit(solution)/shard_map/lic,ib->lbc/dot_general | solution.py:127
  133.0 1.4 reshape.2625
  134.4 1.4 add.2478
  136.0 2.3 %collective-permute-start.4 = (f32[34,1,1024]{2,1,0:T(1,128)S(1)}, f32[34,1,1024]{2,1,0:T(1,128)S(1)}, u32[]{:S(2)}, u32[]{:S(2)}) collective-permute-start(f32[34,1,1024]{2,1,0:T(1,128)S(1)} %get-tuple-element.84), channel_id=1, source_target_pairs={{0,16},{16,32},{32,48},{48,64},{64,80},{80,96},{96,112},{112,128},... | collective-permute-start | bytes 417800 | tf_op jit(solution)/shard_map/ppermute | solution.py:19
  138.3 1.3 collective-permute-start.3
  140.0 1.5 collective-permute-done.3
  141.6 0.7 fusion.13
  142.4 1.7 fusion.175
  144.1 5.1 %collective-permute-start.6 = (f32[17,1,1024]{2,1,0:T(1,128)S(1)}, f32[17,1,1024]{2,1,0:T(1,128)S(1)}, u32[]{:S(2)}, u32[]{:S(2)}) collective-permute-start(f32[17,1,1024]{2,1,0:T(1,128)S(1)} %get-tuple-element.141), channel_id=1, source_target_pairs={{0,16},{16,32},{32,48},{48,64},{64,80},{80,96},{96,112},{112,128},... | collective-permute-start | bytes 208904 | tf_op jit(solution)/shard_map/ppermute | solution.py:19
  149.2 1.3 collective-permute-start.5
  150.5 1.7 fusion.35
  152.2 2.2 %reduce_sum.39 = f32[8,16,1024]{2,1,0:T(8,128)} reduce(f32[2,8,16,1024]{3,2,1,0:T(8,128)} %bitcast.739, f32[]{:T(128)} %constant.27.clone.1), dimensions={0}, to_apply=%region_7.8 | reduce | flops 131072 | bytes 1572868 | tf_op jit(solution)/shard_map/reduce_sum | solution.py:170
  154.7 0.9 copy-done.3
  156.0 0.6 fusion.20
  156.7 3.0 %collective-permute-start.8 = (f32[17,1,1024]{2,1,0:T(1,128)S(1)}, f32[17,1,1024]{2,1,0:T(1,128)S(1)}, u32[]{:S(2)}, u32[]{:S(2)}) collective-permute-start(f32[17,1,1024]{2,1,0:T(1,128)S(1)} %get-tuple-element.139), channel_id=1, source_target_pairs={{0,16},{16,32},{32,48},{48,64},{64,80},{80,96},{96,112},{112,128},... | collective-permute-start | bytes 208904 | tf_op jit(solution)/shard_map/ppermute | solution.py:19
  160.2 1.3 collective-permute-start.7
  161.8 2.3 %collective-permute-done.7 = f32[17,1,1024]{2,1,0:T(1,128)S(1)} collective-permute-done((f32[17,1,1024]{2,1,0:T(1,128)S(1)}, f32[17,1,1024]{2,1,0:T(1,128)S(1)}, u32[]{:S(2)}, u32[]{:S(2)}) %collective-permute-start.7) | collective-permute-done | bytes 69664 | tf_op jit(solution)/shard_map/ppermute | solution.py:21
  164.1 1.6 fusion.27
  165.7 15.6 %reduce-scatter.2.cloned.1.call-done = f32[8,16,256]{2,1,0:T(8,128)} async-done(((f32[8,16,1024]{2,1,0:T(8,128)}), f32[8,16,256]{2,1,0:T(8,128)}) %reduce-scatter.2.cloned.1.call-update) | async-done | bytes 131088 | tf_op jit(solution)/shard_map/reduce_scatter | solution.py:169
  (110 shorter events, 17.5 us)
Async XLA Ops:
  7.2 1.0 copy-start.9
  7.2 1.4 copy-start.1
  8.6 4.8 %copy-start.11 = (s32[16,256]{1,0:T(8,128)S(1)}, s32[16,256]{1,0:T(8,128)}, u32[]{:S(2)}) copy-start(s32[16,256]{1,0:T(8,128)} %param.18) | copy-start | bytes 49156
  9.6 7.2 %copy-start.12 = (s32[16,256]{1,0:T(8,128)S(1)}, s32[16,256]{1,0:T(8,128)}, u32[]{:S(2)}) copy-start(s32[16,256]{1,0:T(8,128)} %param.19) | copy-start | bytes 49156
  9.6 12.6 %collective-permute-start = (f32[3,8,16,256]{3,2,0,1:T(8,128)}, f32[3,8,16,256]{3,2,0,1:T(8,128)}, u32[]{:S(2)}, u32[]{:S(2)}) collective-permute-start(f32[3,8,16,256]{3,2,0,1:T(8,128)} %get-tuple-element.136), channel_id=1, source_target_pairs={{0,4},{4,0},{8,12},{12,8},{1,5},{5,1},{9,13},{13,9},{2,6},{6,2},{1... | collective-permute-start | bytes 1179656 | tf_op jit(solution)/shard_map/ppermute | solution.py:157
  11.9 18.4 %collective-permute-start.1 = (f32[3,8,16,256]{3,2,0,1:T(8,128)}, f32[3,8,16,256]{3,2,0,1:T(8,128)}, u32[]{:S(2)}, u32[]{:S(2)}) collective-permute-start(f32[3,8,16,256]{3,2,0,1:T(8,128)} %get-tuple-element.137), channel_id=1, source_target_pairs={{0,8},{4,12},{8,0},{12,4},{1,9},{5,13},{9,1},{13,5},{2,10},{6,14},... | collective-permute-start | bytes 1179656 | tf_op jit(solution)/shard_map/ppermute | solution.py:157
  12.6 18.7 %collective-permute-start.2 = (f32[3,8,16,256]{3,2,0,1:T(8,128)S(1)}, f32[3,8,16,256]{3,2,0,1:T(8,128)S(1)}, u32[]{:S(2)}, u32[]{:S(2)}) collective-permute-start(f32[3,8,16,256]{3,2,0,1:T(8,128)S(1)} %get-tuple-element.134), channel_id=1, source_target_pairs={{0,12},{4,8},{8,4},{12,0},{1,13},{5,9},{9,5},{13,1},{2,14},{6,10},... | collective-permute-start | bytes 1179656 | tf_op jit(solution)/shard_map/ppermute | solution.py:157
  46.3 12.7 %copy-start.14 = (s32[256,1]{0,1:T(1,128)S(1)}, s32[256,1]{0,1:T(1,128)}, u32[]{:S(2)}) copy-start(s32[256,1]{0,1:T(1,128)} %reshape.2624) | copy-start | bytes 3076
  52.5 18.9 %all-to-all-start = ((f32[2,32,16,256]{3,2,0,1:T(8,128)}), f32[2,32,16,256]{3,2,0,1:T(8,128)S(1)}, u32[]{:S(2)}, u32[]{:S(2)}) async-start(f32[2,32,16,256]{3,2,0,1:T(8,128)} %constant_dynamic-update-slice_fusion), calls=%async_computation | async-start | bytes 2097152 | tf_op jit(solution)/shard_map/all_to_all | solution.py:160
  59.0 2.4 %copy-start.16 = (s32[256]{0:T(256)S(1)}, s32[256]{0:T(256)}, u32[]{:S(2)}) copy-start(s32[256]{0:T(256)} %reshape.2622) | copy-start | bytes 3076
  59.0 2.4 %copy-start.13 = (f32[256]{0:T(256)S(1)}, f32[256]{0:T(256)}, u32[]{:S(2)}) copy-start(f32[256]{0:T(256)} %convert_element_type.43) | copy-start | bytes 3076
  65.1 15.9 %copy-start.15 = (s32[16]{0:T(128)S(1)}, s32[16]{0:T(128)}, u32[]{:S(2)}) copy-start(s32[16]{0:T(128)} %param.21) | copy-start | bytes 196
  65.1 18.7 %copy-start.10 = (f32[16,1024]{1,0:T(8,128)S(1)}, f32[16,1024]{1,0:T(8,128)}, u32[]{:S(2)}) copy-start(f32[16,1024]{1,0:T(8,128)} %param.14) | copy-start | bytes 196612
  65.1 18.8 %copy-start.8 = (f32[16,1024]{1,0:T(8,128)S(1)}, f32[16,1024]{1,0:T(8,128)}, u32[]{:S(2)}) copy-start(f32[16,1024]{1,0:T(8,128)} %param.16) | copy-start | bytes 196612
  71.4 1.0 copy-start.2
  72.4 57.8 %all-to-all-start.1 = ((f32[16,256,128]{2,0,1:T(8,128)}), f32[16,256,128]{2,0,1:T(8,128)S(1)}, u32[]{:S(2)}, u32[]{:S(2)}) async-start(f32[16,256,128]{2,0,1:T(8,128)} %multiply_bitcast_fusion), calls=%async_computation.1 | async-start | bytes 4194304 | tf_op jit(solution)/shard_map/all_to_all | solution.py:109
  81.0 100.3 %reduce-scatter.2.cloned.1.call-start = ((), (), s32[]{:S(2)}) async-start(), calls=%async_computation.3 | async-start | bytes 655360 | tf_op jit(solution)/shard_map/reduce_scatter | solution.py:169
  134.3 1.4 copy-start
  134.4 1.4 copy-start.7
  136.0 4.0 %collective-permute-start.4 = (f32[34,1,1024]{2,1,0:T(1,128)S(1)}, f32[34,1,1024]{2,1,0:T(1,128)S(1)}, u32[]{:S(2)}, u32[]{:S(2)}) collective-permute-start(f32[34,1,1024]{2,1,0:T(1,128)S(1)} %get-tuple-element.84), channel_id=1, source_target_pairs={{0,16},{16,32},{32,48},{48,64},{64,80},{80,96},{96,112},{112,128},... | collective-permute-start | bytes 417800 | tf_op jit(solution)/shard_map/ppermute | solution.py:19
  138.3 3.3 %collective-permute-start.3 = (f32[34,1,1024]{2,1,0:T(1,128)S(1)}, f32[34,1,1024]{2,1,0:T(1,128)S(1)}, u32[]{:S(2)}, u32[]{:S(2)}) collective-permute-start(f32[34,1,1024]{2,1,0:T(1,128)S(1)} %get-tuple-element.83), channel_id=1, source_target_pairs={{16,0},{32,16},{48,32},{64,48},{80,64},{96,80},{112,96},{128,112},... | collective-permute-start | bytes 417800 | tf_op jit(solution)/shard_map/ppermute | solution.py:21
  142.4 8.1 %copy-start.5 = (f32[16,16,1023]{2,1,0:T(8,128)S(1)}, f32[16,16,1023]{2,1,0:T(8,128)}, u32[]{:S(2)}) copy-start(f32[16,16,1023]{2,1,0:T(8,128)} %get-tuple-element.148) | copy-start | bytes 3142660
  142.4 8.1 %copy-start.6 = (f32[16,16,1023]{2,1,0:T(8,128)S(1)}, f32[16,16,1023]{2,1,0:T(8,128)}, u32[]{:S(2)}) copy-start(f32[16,16,1023]{2,1,0:T(8,128)} %get-tuple-element.149) | copy-start | bytes 3142660
  144.1 10.3 %collective-permute-start.6 = (f32[17,1,1024]{2,1,0:T(1,128)S(1)}, f32[17,1,1024]{2,1,0:T(1,128)S(1)}, u32[]{:S(2)}, u32[]{:S(2)}) collective-permute-start(f32[17,1,1024]{2,1,0:T(1,128)S(1)} %get-tuple-element.141), channel_id=1, source_target_pairs={{0,16},{16,32},{32,48},{48,64},{64,80},{80,96},{96,112},{112,128},... | collective-permute-start | bytes 208904 | tf_op jit(solution)/shard_map/ppermute | solution.py:19
  149.2 5.5 %collective-permute-start.5 = (f32[17,1,1024]{2,1,0:T(1,128)S(1)}, f32[17,1,1024]{2,1,0:T(1,128)S(1)}, u32[]{:S(2)}, u32[]{:S(2)}) collective-permute-start(f32[17,1,1024]{2,1,0:T(1,128)S(1)} %get-tuple-element.140), channel_id=1, source_target_pairs={{16,0},{32,16},{48,32},{64,48},{80,64},{96,80},{112,96},{128,112},... | collective-permute-start | bytes 208904 | tf_op jit(solution)/shard_map/ppermute | solution.py:21
  154.4 1.2 copy-start.3
  154.4 1.5 copy-start.4
  156.7 4.7 %collective-permute-start.8 = (f32[17,1,1024]{2,1,0:T(1,128)S(1)}, f32[17,1,1024]{2,1,0:T(1,128)S(1)}, u32[]{:S(2)}, u32[]{:S(2)}) collective-permute-start(f32[17,1,1024]{2,1,0:T(1,128)S(1)} %get-tuple-element.139), channel_id=1, source_target_pairs={{0,16},{16,32},{32,48},{48,64},{64,80},{80,96},{96,112},{112,128},... | collective-permute-start | bytes 208904 | tf_op jit(solution)/shard_map/ppermute | solution.py:19
  160.2 3.9 %collective-permute-start.7 = (f32[17,1,1024]{2,1,0:T(1,128)S(1)}, f32[17,1,1024]{2,1,0:T(1,128)S(1)}, u32[]{:S(2)}, u32[]{:S(2)}) collective-permute-start(f32[17,1,1024]{2,1,0:T(1,128)S(1)} %get-tuple-element.138), channel_id=1, source_target_pairs={{16,0},{32,16},{48,32},{64,48},{80,64},{96,80},{112,96},{128,112},... | collective-permute-start | bytes 208904 | tf_op jit(solution)/shard_map/ppermute | solution.py:21
Sparse Core Ops, SparseCore 0:
  154.6 26.7 reduce-scatter.1
